TPU v7x, 32 devices: a whole 2x2x4 slice. The times are simulated.
32 devices in a mesh: req: 8 (over z, x), head: 4 (over y, core).
Axes of the slice: x: 2, y: 2, z: 4, core: 2. Of those that a mesh axis runs over, the one named last changes fastest.
Arguments:
- query_new: bfloat16 [512, 5120], P('req', 'head'), may hold values from -6 to 6
- key_new: bfloat16 [512, 5120], P('req', 'head'), may hold values from -6 to 6
- value_new: bfloat16 [512, 5120], P('req', 'head'), may hold values from -6 to 6
- key_pool: bfloat16 [28288, 5120], P('req', 'head'), may hold values from -368 to 368
- value_pool: bfloat16 [28288, 5120], P('req', 'head'), may hold values from -6 to 6
- lengths: int32 [512], replicated, may hold values from 8 to 1024, as said below
- slot_request: int32 [512], replicated, may hold values from 0 to 511, as said below
- residual: bfloat16 [512, 5120], P(None, 'req'), may hold values from -6 to 6
- out_proj: bfloat16 [5120, 5120], P('head', 'req'), may hold values from -0.15625 to 0.15625
- norm_gain: bfloat16 [5120], replicated, may hold values from 0.5 to 1.5
- gate_proj: bfloat16 [5120, 13824], P(None, ('req', 'head')), may hold values from -0.078125 to 0.078125
- up_proj: bfloat16 [5120, 13824], P(None, ('req', 'head')), may hold values from -0.078125 to 0.078125
- down_proj: bfloat16 [13824, 5120], P('req', 'head'), may hold values from -0.21875 to 0.21875
Outputs:
- attended: bfloat16 [512, 5120], P('head', 'req')
- ffn_out: bfloat16 [512, 5120], P('req', 'head')
Inputs may be any that keep to these rules, and one draw needn't show every extreme that they name: `slot_request`: a permutation of the requests; the 8 requests with more than 24 cached tokens sit two to an owner, on 4 owners. `lengths`: exactly 8 requests have 1024 // 2 to 1024 cached tokens and one of them has 1024; every other request has 8 to 24.
All inputs are finite; a program needn't handle non-finite values.
Results may differ from a plain program's by a relative error of at most 0.017.
Values may be sent and summed in bfloat16 or wider, within the bound.
A program may use at most 192 MiB of HBM per device.

v0:
```python
import math

import jax
import jax.numpy as jnp
from jax import lax
from jax.sharding import PartitionSpec as P

D = 5120
HD = 128


def rope_tables(positions):
    half_dim = HD // 2
    freq_steps = jnp.arange(half_dim, dtype=jnp.float32)
    inverse = jnp.exp(freq_steps * (-2.0 * math.log(10000.0) / HD))
    angles = positions.astype(jnp.float32)[:, None] * inverse[None, :]
    return (jnp.cos(angles), jnp.sin(angles))


def rotate_half(vectors, cosine, sine_table):
    half_dim = HD // 2
    first_half = vectors[..., :half_dim]
    second = vectors[..., half_dim:]
    cos_grid = cosine[:, None, :]
    sin_grid = sine_table[:, None, :]
    return jnp.concatenate(
        [first_half * cos_grid - second * sin_grid, second * cos_grid + first_half * sin_grid],
        axis=-1,
    )


def attend_local(query_rot, key_rot, value_new, pool_keys, pool_values, seg_lengths):
    score_scale = HD ** (-0.5)
    seg_ends = jnp.cumsum(seg_lengths)
    starts = seg_ends - seg_lengths
    places = jnp.arange(pool_keys.shape[0], dtype=jnp.int32)
    member = (places[None, :] >= starts[:, None]) & (places[None, :] < seg_ends[:, None])
    scores = (
        jnp.einsum("rgd,pgd->grp", query_rot, pool_keys, preferred_element_type=jnp.float32)
        * score_scale
    )
    own_score = (
        jnp.sum(query_rot.astype(jnp.float32) * key_rot.astype(jnp.float32), axis=-1).T
        * score_scale
    )
    masked = jnp.where(member[None], scores, -jnp.inf)
    row_top = jnp.maximum(jnp.max(masked, axis=-1), own_score)
    weights = jnp.where(member[None], jnp.exp(scores - row_top[:, :, None]), 0.0)
    own_weight = jnp.exp(own_score - row_top)
    row_total = jnp.sum(weights, axis=-1) + own_weight
    summed = jnp.einsum(
        "grp,pgd->rgd",
        weights.astype(jnp.bfloat16),
        pool_values,
        preferred_element_type=jnp.float32,
    )
    own_bf = lax.optimization_barrier(own_weight.astype(jnp.bfloat16)).astype(jnp.float32)
    summed = summed + own_bf.T[:, :, None] * value_new.astype(jnp.float32)
    return (summed / row_total.T[:, :, None]).astype(jnp.bfloat16)


def body(
    query_new,
    key_new,
    value_new,
    key_pool,
    value_pool,
    lengths,
    slot_request,
    residual,
    out_proj,
    norm_gain,
    gate_proj,
    up_proj,
    down_proj,
):
    owned = query_new.shape[0]
    groups = query_new.shape[1] // HD
    pool_rows = key_pool.shape[0]
    req_count = lax.axis_size("req")
    head_count = lax.axis_size("head")
    first_slot = lax.axis_index("req") * owned
    my_requests = lax.dynamic_slice_in_dim(slot_request, first_slot, owned, 0)
    my_lengths = jnp.take(lengths, my_requests, axis=0)
    cosine, sine_table = rope_tables(my_lengths)
    shaped = (owned, groups, HD)
    query_rot = rotate_half(
        query_new.astype(jnp.float32).reshape(shaped), cosine, sine_table
    ).astype(jnp.bfloat16)
    key_rot = rotate_half(key_new.astype(jnp.float32).reshape(shaped), cosine, sine_table).astype(
        jnp.bfloat16
    )
    attention = attend_local(
        query_rot,
        key_rot,
        value_new.reshape(shaped),
        key_pool.reshape(pool_rows, groups, HD),
        value_pool.reshape(pool_rows, groups, HD),
        my_lengths,
    ).reshape(owned, groups * HD)
    partial_sums = jnp.dot(
        lax.all_gather(attention, "req", axis=0, tiled=True),
        out_proj,
        preferred_element_type=jnp.float32,
    )
    summed = lax.psum_scatter(partial_sums, "head", scatter_dimension=0, tiled=True)
    quarter = summed.shape[0]
    quarter_slots = lax.dynamic_slice_in_dim(
        slot_request, lax.axis_index("head") * quarter, quarter, 0
    )
    attended = (jnp.take(residual, quarter_slots, axis=0).astype(jnp.float32) + summed).astype(
        jnp.bfloat16
    )
    column_width = attended.shape[1]
    gain_grid = norm_gain.astype(jnp.float32).reshape(req_count, 1, column_width)
    everywhere = lax.all_gather(attended[None], ("req", "head"), axis=0, tiled=True)
    hidden_grid = everywhere.reshape(req_count, head_count, quarter, column_width).astype(
        jnp.float32
    )
    squares = jnp.sum(hidden_grid * hidden_grid, axis=(0, 3))
    inverse = lax.rsqrt(squares / D + 1e-05)
    scaled = (hidden_grid * inverse[None, :, :, None] * gain_grid[:, None]).astype(jnp.bfloat16)
    col_block = gate_proj.shape[1]
    gate_pre = jnp.einsum(
        "rhbc,rcf->hbf",
        scaled,
        gate_proj.reshape(req_count, column_width, col_block),
        preferred_element_type=jnp.float32,
    )
    upward = jnp.einsum(
        "rhbc,rcf->hbf",
        scaled,
        up_proj.reshape(req_count, column_width, col_block),
        preferred_element_type=jnp.float32,
    )
    active = (jax.nn.silu(gate_pre) * upward).astype(jnp.bfloat16)
    gathered = lax.all_gather(active, "head", axis=2, tiled=True)
    active_all = gathered.reshape(head_count * quarter, head_count * col_block)
    ffn_out = lax.psum_scatter(
        jnp.dot(active_all, down_proj, preferred_element_type=jnp.float32).astype(jnp.bfloat16),
        "req",
        scatter_dimension=0,
        tiled=True,
    )
    return (attended, ffn_out)


def solution(mesh):
    placed = (
        P("req", "head"),
        P("req", "head"),
        P("req", "head"),
        P("req", "head"),
        P("req", "head"),
        P(),
        P(),
        P(None, "req"),
        P("head", "req"),
        P(),
        P(None, ("req", "head")),
        P(None, ("req", "head")),
        P("req", "head"),
    )
    return jax.shard_map(
        body,
        mesh=mesh,
        in_specs=placed,
        out_specs=(P("head", "req"), P("req", "head")),
        check_vma=False,
    )
```

profile of v0, /device:TPU:0, one launch (start us, length us, event | category | flops | bytes accessed | tf_op | source)
XLA Modules:
  0.0 320.4 jit_solution(6889549121941848388)
XLA Ops:
  7.2 0.9 compare_select_fusion
  8.1 1.5 gather_fusion.1
  10.4 1.0 reshape.192
  11.4 1.0 reshape.194
  13.0 12.8 %copy.54 = bf16[3536,1280]{0,1:T(8,128)(2,1)} copy(bf16[3536,1280]{1,0:T(8,128)(2,1)} %param.16) | data formatting | bytes 18104320 | tf_op args[3]
  27.1 6.1 %select_reduce_fusion = (f32[10,64]{1,0:T(8,128)S(1)}, f32[10,64,3536]{2,1,0:T(8,128)S(1)}) fusion(pred[64,3536]{1,0:T(8,128)(4,1)S(1)} %fusion.33, bf16[3536,10,128]{0,2,1:T(8,128)(2,1)} %bitcast.90, bf16[64,10,64]{2,0,1:T(8,128)(2,1)S(1)} %get-tuple-element.14, bf16[64,10,64]{2,0,1:T(8,128)(2,1)S(1)} %get-tuple-element.15), kind=kOutput, calls=%fused_computation.7 | convolution fusion | flops 586454400 | bytes 18497024 | tf_op jit(solution)/shard_map/rgd,pgd->grp/dot_general | solution.py:39
  33.2 3.5 %copy-done.1 = f32[10,64,3536]{2,1,0:T(8,128)} copy-done((f32[10,64,3536]{2,1,0:T(8,128)}, f32[10,64,3536]{2,1,0:T(8,128)S(1)}, u32[]{:S(2)}) %copy-start.1) | copy-done | bytes 9052184
  36.8 2.3 fusion.2
  39.1 12.8 %copy.58 = bf16[3536,1280]{0,1:T(8,128)(2,1)} copy(bf16[3536,1280]{1,0:T(8,128)(2,1)} %param.17) | data formatting | bytes 18104320 | tf_op args[4]
  52.0 9.6 %fusion.30 = bf16[10,8,8,128]{3,2,1,0:T(8,128)(2,1)S(1)} fusion(bf16[3536,10,128]{0,2,1:T(8,128)(2,1)} %bitcast.91, f32[10,64,3536]{2,1,0:T(8,128)} %copy-done.1, f32[10,64]{1,0:T(8,128)S(1)} %get-tuple-element.17, pred[64,3536]{1,0:T(8,128)(4,1)S(1)} %fusion.33, f32[64,10]{0,1:T(8,128)S(1)} %fusion.38, f32[64,10]{0,1:T(8,128)S(1)} %convert_bitcast_fusion.1, ...), kind=kOutput, calls=%fused_computation.30 | convolution fusion | flops 588800000 | bytes 18665984 | tf_op jit(solution)/shard_map/grp,pgd->rgd/dot_general | solution.py:51
  62.3 44.9 %all-gather.5.cloned.1.call-done = bf16[512,1280]{1,0:T(8,128)(2,1)} async-done(((bf16[64,1280]{1,0:T(8,128)(2,1)}), bf16[512,1280]{1,0:T(8,128)(2,1)}) %all-gather.5.cloned.1.call-update) | async-done | bytes 1310736 | tf_op jit(solution)/shard_map/all_gather | solution.py:102
  107.2 3.6 %fusion.47 = f32[512,640]{1,0:T(8,128)} fusion(bf16[512,1280]{1,0:T(8,128)(2,1)} %all-gather.5.cloned.1.call-done, bf16[1280,640]{1,0:T(8,128)(2,1)S(1)} %copy-done), kind=kOutput, calls=%fused_computation.69 | convolution fusion | flops 838860800 | bytes 4259840 | tf_op jit(solution)/shard_map/dot_general | solution.py:101
  110.8 0.8 compare_and_fusion
  111.6 0.9 gather_fusion
  112.5 23.6 %reduce-scatter.3.cloned.1.call-done = f32[128,640]{1,0:T(8,128)} async-done(((f32[512,640]{1,0:T(8,128)}), f32[128,640]{1,0:T(8,128)}) %reduce-scatter.3.cloned.1.call-update) | async-done | bytes 327696 | tf_op jit(solution)/shard_map/reduce_scatter | solution.py:106
  136.1 1.7 add_convert_fusion
  138.2 67.1 %all-gather.9.cloned.1.call-done = bf16[4096,640]{1,0:T(8,128)(2,1)} async-done(((bf16[128,640]{1,0:T(8,128)(2,1)}), bf16[4096,640]{1,0:T(8,128)(2,1)}) %all-gather.9.cloned.1.call-update) | async-done | bytes 5242896 | tf_op jit(solution)/shard_map/all_gather | solution.py:116
  205.3 3.7 %multiply_reduce_fusion = f32[4096]{0:T(1024)S(1)} fusion(bf16[4096,640]{1,0:T(8,128)(2,1)} %all-gather.9.cloned.1.call-done), kind=kLoop, calls=%fused_computation.5 | loop fusion | flops 7860224 | bytes 5259264 | tf_op jit(solution)/shard_map/reduce_sum | solution.py:120
  209.0 6.2 %fusion.14 = f32[4,128,432]{1,2,0:T(8,128)S(1)} fusion(bf16[54,8,8,640]{3,2,1,0:T(8,128)(2,1)} %bitcast.100, f32[8,640]{1,0:T(8,128)S(1)} %reshape.197, f32[4,128]{1,0:T(4,128)S(1)} %add_rsqrt_fusion, bf16[8,4,128,640]{3,2,1,0:T(8,128)(2,1)} %bitcast.92), kind=kOutput, calls=%fused_computation.22 | convolution fusion | flops 2275409920 | bytes 10573824 | tf_op jit(solution)/shard_map/rhbc,rcf->hbf/dot_general | solution.py:124
  215.2 5.7 %fusion.17 = bf16[4,128,432]{1,2,0:T(8,128)(2,1)} fusion(bf16[54,8,8,640]{3,2,1,0:T(8,128)(2,1)} %bitcast.101, f32[4,128,432]{1,2,0:T(8,128)S(1)} %fusion.14, f32[8,640]{1,0:T(8,128)S(1)} %reshape.197, f32[4,128]{1,0:T(4,128)S(1)} %add_rsqrt_fusion, bf16[8,4,128,640]{3,2,1,0:T(8,128)(2,1)S(1)} %bitcast.95), kind=kOutput, calls=%fused_computation.25 | convolution fusion | flops 2276737024 | bytes 11016192 | tf_op jit(solution)/shard_map/rhbc,rcf->hbf/dot_general | solution.py:130
  221.0 19.7 %all-gather.7.cloned.1.call-done = bf16[4,128,1728]{1,2,0:T(8,128)(2,1)} async-done(((bf16[4,128,432]{1,2,0:T(8,128)(2,1)}), bf16[4,128,1728]{1,2,0:T(8,128)(2,1)}) %all-gather.7.cloned.1.call-update) | async-done | bytes 1769488 | tf_op jit(solution)/shard_map/all_gather | solution.py:137
  240.7 2.8 copy.66
  243.5 5.9 %convolution_convert_fusion = bf16[512,1280]{1,0:T(8,128)(2,1)} fusion(bf16[512,1728]{1,0:T(8,128)(2,1)S(1)} %bitcast.96, bf16[1728,1280]{1,0:T(8,128)(2,1)} %param.25), kind=kOutput, calls=%fused_computation.21 | convolution fusion | flops 2265579520 | bytes 7503872 | tf_op jit(solution)/shard_map/dot_general | solution.py:140
  249.4 64.5 %reduce-scatter.5.cloned.1.call-done = bf16[64,1280]{1,0:T(8,128)(2,1)} async-done(((bf16[512,1280]{1,0:T(8,128)(2,1)}), bf16[64,1280]{1,0:T(8,128)(2,1)}) %reduce-scatter.5.cloned.1.call-update) | async-done | bytes 163856 | tf_op jit(solution)/shard_map/reduce_scatter | solution.py:139
  (44 shorter events, 3.9 us)
Async XLA Ops:
  7.2 100.0 %copy-start = (bf16[1280,640]{1,0:T(8,128)(2,1)S(1)}, bf16[1280,640]{1,0:T(8,128)(2,1)}, u32[]{:S(2)}) copy-start(bf16[1280,640]{1,0:T(8,128)(2,1)} %param.21) | copy-start | bytes 4915204
  7.2 100.0 %all-gather.5.cloned.1.call-start = ((), (), s32[]{:S(2)}) async-start(), calls=%async_computation.2 | async-start | bytes 1474560 | tf_op jit(solution)/shard_map/all_gather | solution.py:102
  33.2 3.6 %copy-start.1 = (f32[10,64,3536]{2,1,0:T(8,128)}, f32[10,64,3536]{2,1,0:T(8,128)S(1)}, u32[]{:S(2)}) copy-start(f32[10,64,3536]{2,1,0:T(8,128)S(1)} %get-tuple-element.21) | copy-start | bytes 27156484
  39.1 12.9 %copy-start.4 = (bf16[64,1280]{1,0:T(8,128)(2,1)S(1)}, bf16[64,1280]{1,0:T(8,128)(2,1)}, u32[]{:S(2)}) copy-start(bf16[64,1280]{1,0:T(8,128)(2,1)} %param.15) | copy-start | bytes 491524
  61.5 50.1 %copy-start.2 = (bf16[512,640]{1,0:T(8,128)(2,1)S(1)}, bf16[512,640]{1,0:T(8,128)(2,1)}, u32[]{:S(2)}) copy-start(bf16[512,640]{1,0:T(8,128)(2,1)} %param.20) | copy-start | bytes 1966084
  61.5 76.6 %copy-start.3 = (bf16[5120]{0:T(1024)(128)(2,1)S(1)}, bf16[5120]{0:T(1024)(128)(2,1)}, u32[]{:S(2)}) copy-start(bf16[5120]{0:T(1024)(128)(2,1)} %param.22) | copy-start | bytes 30724
  62.3 73.9 %reduce-scatter.3.cloned.1.call-start = ((), (), s32[]{:S(2)}) async-start(), calls=%async_computation.3 | async-start | bytes 1638400 | tf_op jit(solution)/shard_map/reduce_scatter | solution.py:106
  110.8 94.5 %all-gather.9.cloned.1.call-start = ((), (), s32[]{:S(2)}) async-start(), calls=%async_computation.6 | async-start | bytes 5406720 | tf_op jit(solution)/shard_map/all_gather | solution.py:116
  137.9 102.8 %all-gather.7.cloned.1.call-start = ((), (), s32[]{:S(2)}) async-start(), calls=%async_computation.4 | async-start | bytes 2211840 | tf_op jit(solution)/shard_map/all_gather | solution.py:137
  205.3 9.9 %slice-start = ((s8[5242880]{0:T(1024)(128)(4,1)}), s8[1048576]{0:T(1024)(128)(4,1)S(1)}, s32[]{:S(2)}) async-start(s8[5242880]{0:T(1024)(128)(4,1)} %bitcast.93), calls=%async_computation.7 | async-start | bytes 2097152
  209.0 6.2 %slice-start.1 = ((s8[5242880]{0:T(1024)(128)(4,1)}), s8[4194304]{0:T(1024)(128)(4,1)S(1)}, s32[]{:S(2)}) async-start(s8[5242880]{0:T(1024)(128)(4,1)} %bitcast.93), calls=%async_computation.8 | async-start | bytes 8388608
  220.9 92.9 %reduce-scatter.5.cloned.1.call-start = ((), (), s32[]{:S(2)}) async-start(), calls=%async_computation.5 | async-start | bytes 1474560 | tf_op jit(solution)/shard_map/reduce_scatter | solution.py:139
Sparse Core Ops, SparseCore 0:
  62.4 44.7 all-gather.4
  110.9 25.1 reduce-scatter.2
  139.9 65.2 all-gather.8
  221.1 19.6 all-gather.6
  249.5 64.3 reduce-scatter.4
where the time goes:
time: 321 us; the launch traced here: 320 us
  waiting for transfers between devices  220 us (69%)
  local copies, waits for them, and re-layouts  37.5 us (12%)
  matrix products  37 us (12%)
  between operations  14 us (4%)
  other arithmetic  11.6 us (4%)
    all_gather x1, waiting for transfers between devices, body(): lax.all_gather(attended[None], ('req', 'head'), axis=0, tiled=True)  67.1 us
    reduce_scatter x1, waiting for transfers between devices, body(): lax.psum_scatter(jnp.dot(active_all, down_proj, preferred_element_type=jn...  64.5 us
    all_gather x1, waiting for transfers between devices, body(): lax.all_gather(attention, 'req', axis=0, tiled=True)  44.9 us
    unnamed x16, local copies, waits for them, and re-layouts  29.2 us
    reduce_scatter x1, waiting for transfers between devices, body(): lax.psum_scatter(partial_sums, 'head', scatter_dimension=0, tiled=True)  23.6 us
    all_gather x1, waiting for transfers between devices, body(): gathered = lax.all_gather(active, 'head', axis=2, tiled=True)  19.7 us
    dot_general x1, matrix products, attend_local(): jnp.einsum('grp,pgd->rgd', weights.astype(jnp.bfloat16), pool_values, pre...  9.56 us
  transfers between devices with their start and end apart: 5, of which 5 were waited for; matrix products, arithmetic and copies ran while one was open for 1% of the time, Pallas kernels for 0%

commit v1 on v0

v1 whole, which is shorter than its diff:
```python
import math

import jax
import jax.numpy as jnp
from jax import lax
from jax.experimental import pallas as pl
from jax.experimental.pallas import tpu as pltpu
from jax.sharding import PartitionSpec as P

D = 5120
HD = 128


def rope_tables(positions):
    half_dim = HD // 2
    freq_steps = jnp.arange(half_dim, dtype=jnp.float32)
    inverse = jnp.exp(freq_steps * (-2.0 * math.log(10000.0) / HD))
    angles = positions.astype(jnp.float32)[:, None] * inverse[None, :]
    return (jnp.cos(angles), jnp.sin(angles))


def swap_halves(v):
    half = HD // 2
    return jnp.concatenate([v[:, half:], v[:, :half]], axis=1)


def attend_kernel(q_ref, k_ref, v_ref, kp_ref, vp_ref, cos_ref, sin_ref, st_ref, en_ref, out_ref):
    scale = HD ** (-0.5)
    owned = q_ref.shape[0]
    rows = kp_ref.shape[0]
    cosine = cos_ref[...]
    sine = sin_ref[...]
    rotated = []
    own = []
    for j in range(2):
        cols = slice(j * HD, (j + 1) * HD)
        q = q_ref[:, cols].astype(jnp.float32)
        k = k_ref[:, cols].astype(jnp.float32)
        q = (q * cosine + swap_halves(q) * sine).astype(jnp.bfloat16)
        k = (k * cosine + swap_halves(k) * sine).astype(jnp.bfloat16)
        rotated.append(q)
        own.append(
            jnp.sum(q.astype(jnp.float32) * k.astype(jnp.float32), axis=-1, keepdims=True) * scale
        )
    blank = jnp.zeros((owned, HD), jnp.bfloat16)
    both = jnp.concatenate(
        [
            jnp.concatenate([rotated[0], blank], axis=1),
            jnp.concatenate([blank, rotated[1]], axis=1),
        ],
        axis=0,
    )
    own = jnp.concatenate(own, axis=0)
    scores = (
        lax.dot_general(
            both, kp_ref[...], (((1,), (1,)), ((), ())), preferred_element_type=jnp.float32
        )
        * scale
    )
    starts = jnp.concatenate([st_ref[...]] * 2, axis=0)
    ends = jnp.concatenate([en_ref[...]] * 2, axis=0)
    places = lax.broadcasted_iota(jnp.int32, (2 * owned, rows), 1)
    member = (places >= starts) & (places < ends)
    masked = jnp.where(member, scores, -jnp.inf)
    top = jnp.maximum(jnp.max(masked, axis=-1, keepdims=True), own)
    weights = jnp.exp(masked - top)
    own_weight = jnp.exp(own - top)
    total = jnp.sum(weights, axis=-1, keepdims=True) + own_weight
    summed = jnp.dot(
        weights.astype(jnp.bfloat16), vp_ref[...], preferred_element_type=jnp.float32
    )
    own_weight = own_weight.astype(jnp.bfloat16).astype(jnp.float32)
    for j in range(2):
        cols = slice(j * HD, (j + 1) * HD)
        part = slice(j * owned, (j + 1) * owned)
        value = v_ref[:, cols].astype(jnp.float32)
        out_ref[:, cols] = (
            (summed[part, cols] + own_weight[part] * value) / total[part]
        ).astype(jnp.bfloat16)


def attend_local(query_new, key_new, value_new, key_pool, value_pool, seg_lengths):
    owned, width = query_new.shape
    rows = key_pool.shape[0]
    cosine, sine = rope_tables(seg_lengths)
    cosine = jnp.concatenate([cosine, cosine], axis=1)
    sine = jnp.concatenate([-sine, sine], axis=1)
    ends = jnp.cumsum(seg_lengths)
    starts = ends - seg_lengths
    wide = 2 * HD
    slots = pl.BlockSpec((owned, wide), lambda i: (0, i))
    pool = pl.BlockSpec((rows, wide), lambda i: (0, i))
    table = pl.BlockSpec((owned, HD), lambda i: (0, 0))
    edge = pl.BlockSpec((owned, 1), lambda i: (0, 0))
    return pl.pallas_call(
        attend_kernel,
        grid=(width // wide,),
        in_specs=[slots, slots, slots, pool, pool, table, table, edge, edge],
        out_specs=slots,
        out_shape=jax.ShapeDtypeStruct((owned, width), jnp.bfloat16),
        compiler_params=pltpu.CompilerParams(vmem_limit_bytes=48 * 1024 * 1024),
        cost_estimate=pl.CostEstimate(
            flops=4 * owned * rows * width,
            bytes_accessed=4 * rows * width,
            transcendentals=owned * rows * width // HD,
        ),
    )(
        query_new,
        key_new,
        value_new,
        key_pool,
        value_pool,
        cosine,
        sine,
        starts[:, None],
        ends[:, None],
    )


def dot_turned(left, right):
    return lax.dot_general(
        left, right, (((1,), (1,)), ((), ())), preferred_element_type=jnp.float32
    )


def layer_kernel(
    att_ref,
    res_ref,
    gain_ref,
    out_hbm,
    gate_hbm,
    up_hbm,
    down_hbm,
    attended_ref,
    ffn_ref,
    wo,
    wg,
    wu,
    wd,
    att_all,
    part,
    core_out,
    core_in,
    y_out,
    y_in,
    hidden,
    squares,
    acc_gate,
    acc_up,
    active,
    down_part,
    x_out,
    x_in,
    z_out,
    z_in,
    w_sem,
    a_zs,
    a_zr,
    a_xs,
    a_xr,
    c_s,
    c_r,
    p_s,
    p_r,
    h_zs,
    h_zr,
    h_xs,
    h_xr,
    h_ys,
    h_yr,
    h_as,
    h_ar,
    h_bs,
    h_br,
    h_cs,
    h_cr,
    g_ys,
    g_yr,
    g_cs,
    g_cr,
    f_xs,
    f_xr,
    f_zs,
    f_zr,
):
    r = lax.axis_index("req")
    h = lax.axis_index("head")
    z = r // 2
    x = r % 2
    y = h // 2
    c = h % 2
    xn = 1 - x
    yn = 1 - y
    cn = 1 - c
    zs = [(z + k) % 4 for k in range(4)]
    to_x = (z * 2 + xn, h)
    to_y = (r, yn * 2 + c)
    to_c = (r, y * 2 + cn)
    to_z = [(zs[k] * 2 + x, h) for k in range(4)]
    f32 = jnp.float32
    bf16 = jnp.bfloat16
    sent = []

    def copy(src, dst, send_sem, recv_sem, device):
        return pltpu.make_async_remote_copy(
            src_ref=src,
            dst_ref=dst,
            send_sem=send_sem,
            recv_sem=recv_sem,
            device_id=device,
            device_id_type=pl.DeviceIdType.MESH,
        )

    def send(*args):
        one = copy(*args)
        one.start()
        sent.append(one)

    def arrived(dst, send_sem, recv_sem, device):
        copy(dst, dst, send_sem, recv_sem, device).wait_recv()

    loads = [
        pltpu.make_async_copy(src, dst, w_sem.at[i])
        for i, (src, dst) in enumerate(
            ((out_hbm, wo), (gate_hbm, wg), (up_hbm, wu), (down_hbm, wd))
        )
    ]
    for load in loads:
        load.start()

    barrier = pltpu.get_barrier_semaphore()
    for device in (to_z[1], to_z[2], to_z[3], to_x, to_y, to_c):
        pl.semaphore_signal(
            barrier, inc=1, device_id=device, device_id_type=pl.DeviceIdType.MESH
        )
    pl.semaphore_wait(barrier, 6)

    for k in (2, 1, 3):
        send(att_ref, att_all.at[r], a_zs.at[k], a_zr.at[z], to_z[k])
    send(att_ref, att_all.at[r], a_xs.at[z], a_xr.at[z], to_x)
    att_all[r] = att_ref[...]
    loads[0].wait()
    for k in (0, 1, 3, 2):
        q = zs[k]
        if k:
            mine = att_all.at[q * 2 + x]
            arrived(mine, a_zs.at[k], a_zr.at[q], to_z[k])
            send(mine, mine, a_xs.at[q], a_xr.at[q], to_x)
    for k in (0, 1, 3, 2):
        q = zs[k]
        arrived(att_all.at[q * 2 + xn], a_xs.at[q], a_xr.at[q], to_x)
        pair = att_all[pl.ds(q * 2, 2)].reshape(part.shape[1], att_ref.shape[1])
        part[q] = jnp.dot(pair, wo[...], preferred_element_type=f32)

    for qy in (yn, y):
        core_out[qy] = part[qy * 2 + cn].astype(bf16)
        send(core_out.at[qy], core_in.at[qy], c_s.at[qy], c_r.at[qy], to_c)
    arrived(core_in.at[yn], c_s.at[yn], c_r.at[yn], to_c)
    y_out[...] = (part[yn * 2 + c] + core_in[yn].astype(f32)).astype(bf16)
    send(y_out, y_in, p_s, p_r, to_y)
    arrived(core_in.at[y], c_s.at[y], c_r.at[y], to_c)
    total = part[h] + core_in[y].astype(f32) + res_ref[...].astype(f32)
    arrived(y_in, p_s, p_r, to_y)
    mine = (total + y_in[...].astype(f32)).astype(bf16)
    attended_ref[...] = mine
    quarter = mine.shape[0]
    half = quarter // 2
    hidden[r, pl.ds(h * quarter, quarter), :] = mine

    def chunk(q, cx, cy, cc):
        return hidden.at[q * 2 + cx, pl.ds((cy * 2 + cc) * quarter, quarter), :]

    def halved(q, cx, cy, cc, which):
        return hidden.at[
            q * 2 + cx, pl.ds((cy * 2 + cc) * quarter + which * half, half), :
        ]

    def to_core(block, q, i):
        send(block, block, h_cs.at[q * 5 + i], h_cr.at[q * 5 + i], to_c)

    def from_core(block, q, i):
        arrived(block, h_cs.at[q * 5 + i], h_cr.at[q * 5 + i], to_c)

    def spread(k):
        q = zs[k]
        block = chunk(q, x, y, c)
        if k:
            arrived(block, h_zs.at[k], h_zr.at[q], to_z[k])
        send(block, block, h_xs.at[q], h_xr.at[q], to_x)
        send(block, block, h_ys.at[q], h_yr.at[q], to_y)
        to_core(block, q, 0)

    def diagonal(k):
        q = zs[k]
        block = chunk(q, xn, y, c)
        arrived(block, h_xs.at[q], h_xr.at[q], to_x)
        piece = halved(q, xn, y, c, 1)
        send(piece, piece, h_bs.at[q], h_br.at[q], to_y)
        to_core(block, q, 1)
        block = chunk(q, x, yn, c)
        arrived(block, h_ys.at[q], h_yr.at[q], to_y)
        piece = halved(q, x, yn, c, 0)
        send(piece, piece, h_as.at[q], h_ar.at[q], to_x)
        to_core(block, q, 2)

    def finish(k):
        q = zs[k]
        piece = halved(q, xn, yn, c, 0)
        arrived(piece, h_as.at[q], h_ar.at[q], to_x)
        to_core(piece, q, 3)
        piece = halved(q, xn, yn, c, 1)
        arrived(piece, h_bs.at[q], h_br.at[q], to_y)
        to_core(piece, q, 4)

    def collect(k):
        q = zs[k]
        from_core(chunk(q, x, y, cn), q, 0)
        from_core(chunk(q, xn, y, cn), q, 1)
        from_core(chunk(q, x, yn, cn), q, 2)
        from_core(halved(q, xn, yn, cn, 0), q, 3)
        from_core(halved(q, xn, yn, cn, 1), q, 4)

    width = mine.shape[1]
    tall = 2 * quarter

    def multiply(k):
        q = zs[k]

        def step(i, carry):
            rows = pl.ds(pl.multiple_of(i * tall, tall), tall)
            gate = up = square = None
            for cx in range(2):
                at = q * 2 + cx
                wide = hidden[at, rows, :].astype(f32)
                power = wide * wide
                for j in range(width // 128):
                    one = power[:, j * 128 : (j + 1) * 128]
                    square = one if square is None else square + one
                scaled = (wide * gain_ref[at]).astype(bf16)
                depth = pl.ds(pl.multiple_of(at * width, width), width)
                one = dot_turned(scaled, wg[:, depth])
                gate = one if gate is None else gate + one
                one = dot_turned(scaled, wu[:, depth])
                up = one if up is None else up + one
            if k == first:
                acc_gate[rows, :] = gate
                acc_up[rows, :] = up
                squares[rows, :] = square
            else:
                acc_gate[rows, :] += gate
                acc_up[rows, :] += up
                squares[rows, :] += square
            return carry

        lax.fori_loop(0, hidden.shape[1] // tall, step, 0)

    own_chunk = chunk(z, x, y, c)
    for k in (2, 1, 3):
        send(own_chunk, own_chunk, h_zs.at[k], h_zr.at[z], to_z[k])
    order = (0, 1, 3, 2)
    first = order[0]
    spread(order[0])
    loads[1].wait()
    loads[2].wait()
    for i in range(4):
        if i < 3:
            spread(order[i + 1])
        diagonal(order[i])
        if i:
            collect(order[i - 1])
            multiply(order[i - 1])
        finish(order[i])
    collect(order[3])
    multiply(order[3])

    def rows_of(q):
        return pl.ds(pl.multiple_of(q * quarter, quarter), quarter)

    late = (1, 3, 2, 0)
    hy = yn * 2 + c
    hc = y * 2 + cn
    hd = yn * 2 + cn
    for k in late:
        q = zs[k]
        mean = jnp.sum(squares[rows_of(q), :], axis=-1, keepdims=True) / D
        inverse = lax.rsqrt(mean + 1e-05)
        gate = acc_gate[rows_of(q), :] * inverse
        up = acc_up[rows_of(q), :] * inverse
        active[h, q] = (gate / (1.0 + jnp.exp(-gate)) * up).astype(bf16)
        block = active.at[h, q]
        send(block, block, g_ys.at[q], g_yr.at[q], to_y)
        send(block, block, g_cs.at[q], g_cr.at[q], to_c)
    loads[3].wait()
    units = active.shape[3]

    def reduce_x(k):
        q = zs[k]
        arrived(x_in.at[q], f_xs.at[q], f_xr.at[q], to_x)
        total = down_part[q, x] + x_in[q].astype(f32)
        if k:
            z_out[q] = total.astype(bf16)
            send(z_out.at[q], z_in.at[z], f_zs.at[q], f_zr.at[z], to_z[k])
            return None
        return total

    for i, k in enumerate(late):
        q = zs[k]
        block = active.at[hy, q]
        arrived(block, g_ys.at[q], g_yr.at[q], to_y)
        send(block, block, g_cs.at[4 + q], g_cr.at[4 + q], to_c)
        arrived(active.at[hc, q], g_cs.at[q], g_cr.at[q], to_c)
        arrived(active.at[hd, q], g_cs.at[4 + q], g_cr.at[4 + q], to_c)
        total = None
        for g in range(4):
            one = jnp.dot(
                active[g, q], wd[g * units : (g + 1) * units, :], preferred_element_type=f32
            )
            total = one if total is None else total + one
        down_part[q] = total.reshape(down_part.shape[1:])
        x_out[q] = down_part[q, xn].astype(bf16)
        send(x_out.at[q], x_in.at[q], f_xs.at[q], f_xr.at[q], to_x)
        if i:
            reduce_x(late[i - 1])
    total = reduce_x(0)
    for k in (1, 3, 2):
        arrived(z_in.at[zs[k]], f_zs.at[zs[k]], f_zr.at[zs[k]], to_z[k])
        total = total + z_in[zs[k]].astype(f32)
    ffn_ref[...] = total.astype(bf16)
    for one in sent:
        one.wait_send()


def layer_local(attention, rows, out_proj, norm_gain, gate_proj, up_proj, down_proj):
    owned, feats = attention.shape
    quarter, width = rows.shape
    gate_proj = gate_proj.T
    up_proj = up_proj.T
    units, hid = gate_proj.shape
    deep, cols = down_proj.shape
    blocks = hid // width
    bf16 = jnp.bfloat16
    f32 = jnp.float32
    dma = pltpu.SemaphoreType.DMA
    vmem = pl.BlockSpec(memory_space=pltpu.VMEM)
    hbm = pl.BlockSpec(memory_space=pl.ANY)
    gain = norm_gain.astype(f32).reshape(blocks, 1, width)
    return pl.pallas_call(
        layer_kernel,
        out_shape=(
            jax.ShapeDtypeStruct((quarter, width), bf16),
            jax.ShapeDtypeStruct((owned, cols), bf16),
        ),
        in_specs=[vmem, vmem, vmem, hbm, hbm, hbm, hbm],
        out_specs=(vmem, vmem),
        scratch_shapes=[
            pltpu.VMEM(out_proj.shape, bf16),
            pltpu.VMEM(gate_proj.shape, bf16),
            pltpu.VMEM(up_proj.shape, bf16),
            pltpu.VMEM(down_proj.shape, bf16),
            pltpu.VMEM((8, owned, feats), bf16),
            pltpu.VMEM((4, quarter, width), f32),
            pltpu.VMEM((2, quarter, width), bf16),
            pltpu.VMEM((2, quarter, width), bf16),
            pltpu.VMEM((quarter, width), bf16),
            pltpu.VMEM((quarter, width), bf16),
            pltpu.VMEM((blocks, 4 * quarter, width), bf16),
            pltpu.VMEM((4 * quarter, 128), f32),
            pltpu.VMEM((4 * quarter, units), f32),
            pltpu.VMEM((4 * quarter, units), f32),
            pltpu.VMEM((4, 4, quarter, units), bf16),
            pltpu.VMEM((4, 2, owned, cols), f32),
            pltpu.VMEM((4, owned, cols), bf16),
            pltpu.VMEM((4, owned, cols), bf16),
            pltpu.VMEM((4, owned, cols), bf16),
            pltpu.VMEM((4, owned, cols), bf16),
            dma((4,)),
            dma((4,)),
            dma((4,)),
            dma((4,)),
            dma((4,)),
            dma((2,)),
            dma((2,)),
            dma,
            dma,
            dma((4,)),
            dma((4,)),
            dma((4,)),
            dma((4,)),
            dma((4,)),
            dma((4,)),
            dma((4,)),
            dma((4,)),
            dma((4,)),
            dma((4,)),
            dma((20,)),
            dma((20,)),
            dma((4,)),
            dma((4,)),
            dma((8,)),
            dma((8,)),
            dma((4,)),
            dma((4,)),
            dma((4,)),
            dma((4,)),
        ],
        compiler_params=pltpu.CompilerParams(
            collective_id=1, has_side_effects=True, vmem_limit_bytes=58 * 1024 * 1024
        ),
        cost_estimate=pl.CostEstimate(
            flops=2 * 4 * quarter * (2 * hid * units + deep * cols + feats * width),
            bytes_accessed=2 * (2 * hid * units + deep * cols + feats * width),
            transcendentals=4 * quarter * units,
        ),
    )(attention, rows, gain, out_proj, gate_proj, up_proj, down_proj)


def body(
    query_new,
    key_new,
    value_new,
    key_pool,
    value_pool,
    lengths,
    slot_request,
    residual,
    out_proj,
    norm_gain,
    gate_proj,
    up_proj,
    down_proj,
):
    owned = query_new.shape[0]
    req_count = lax.axis_size("req")
    head_count = lax.axis_size("head")
    first_slot = lax.axis_index("req") * owned
    my_requests = lax.dynamic_slice_in_dim(slot_request, first_slot, owned, 0)
    my_lengths = jnp.take(lengths, my_requests, axis=0)
    attention = attend_local(query_new, key_new, value_new, key_pool, value_pool, my_lengths)
    if (req_count, head_count) == (8, 4):
        quarter = slot_request.shape[0] // head_count
        quarter_slots = lax.dynamic_slice_in_dim(
            slot_request, lax.axis_index("head") * quarter, quarter, 0
        )
        return layer_local(
            attention,
            jnp.take(residual, quarter_slots, axis=0),
            out_proj,
            norm_gain,
            gate_proj,
            up_proj,
            down_proj,
        )
    partial_sums = jnp.dot(
        lax.all_gather(attention, "req", axis=0, tiled=True),
        out_proj,
        preferred_element_type=jnp.float32,
    )
    summed = lax.psum_scatter(partial_sums, "head", scatter_dimension=0, tiled=True)
    quarter = summed.shape[0]
    quarter_slots = lax.dynamic_slice_in_dim(
        slot_request, lax.axis_index("head") * quarter, quarter, 0
    )
    attended = (jnp.take(residual, quarter_slots, axis=0).astype(jnp.float32) + summed).astype(
        jnp.bfloat16
    )
    column_width = attended.shape[1]
    gain_grid = norm_gain.astype(jnp.float32).reshape(req_count, 1, column_width)
    everywhere = lax.all_gather(attended[None], ("req", "head"), axis=0, tiled=True)
    hidden_grid = everywhere.reshape(req_count, head_count, quarter, column_width).astype(
        jnp.float32
    )
    squares = jnp.sum(hidden_grid * hidden_grid, axis=(0, 3))
    inverse = lax.rsqrt(squares / D + 1e-05)
    scaled = (hidden_grid * inverse[None, :, :, None] * gain_grid[:, None]).astype(jnp.bfloat16)
    col_block = gate_proj.shape[1]
    gate_pre = jnp.einsum(
        "rhbc,rcf->hbf",
        scaled,
        gate_proj.reshape(req_count, column_width, col_block),
        preferred_element_type=jnp.float32,
    )
    upward = jnp.einsum(
        "rhbc,rcf->hbf",
        scaled,
        up_proj.reshape(req_count, column_width, col_block),
        preferred_element_type=jnp.float32,
    )
    active = (jax.nn.silu(gate_pre) * upward).astype(jnp.bfloat16)
    gathered = lax.all_gather(active, "head", axis=2, tiled=True)
    active_all = gathered.reshape(head_count * quarter, head_count * col_block)
    ffn_out = lax.psum_scatter(
        jnp.dot(active_all, down_proj, preferred_element_type=jnp.float32).astype(jnp.bfloat16),
        "req",
        scatter_dimension=0,
        tiled=True,
    )
    return (attended, ffn_out)


def solution(mesh):
    placed = (
        P("req", "head"),
        P("req", "head"),
        P("req", "head"),
        P("req", "head"),
        P("req", "head"),
        P(),
        P(),
        P(None, "req"),
        P("head", "req"),
        P(),
        P(None, ("req", "head")),
        P(None, ("req", "head")),
        P("req", "head"),
    )
    return jax.shard_map(
        body,
        mesh=mesh,
        in_specs=placed,
        out_specs=(P("head", "req"), P("req", "head")),
        check_vma=False,
    )
```

time: 321 us -> 134 us (0.42)
  waiting for transfers between devices: 220 us -> 0 us
  Pallas kernels: 0 us -> 118 us
  matrix products: 37 us -> 0 us
  local copies, waits for them, and re-layouts: 37.5 us -> 9.15 us
  between operations: 14 us -> 0.71 us
  other arithmetic: 11.6 us -> 4.94 us
    all_gather x3 -> x0, waiting for transfers between devices: 132 us -> none  [the longest x1 67.1 us: body(): lax.all_gather(attended[None], ('req', 'head'), axis=0, tiled=True)]
    pallas_call x0 -> x2, Pallas kernels: none -> 118 us  [the longest x1 107 us: layer_local(): pl.pallas_call(layer_kernel, out_shape=(jax.ShapeDtypeStruct((quarter, wi...]
    reduce_scatter x2 -> x0, waiting for transfers between devices: 88.1 us -> none  [the longest x1 64.5 us: body(): lax.psum_scatter(jnp.dot(active_all, down_proj, preferred_element_type=jn...]
    dot_general x6 -> x0, matrix products: 37 us -> none  [the longest x1 9.56 us: attend_local(): jnp.einsum('grp,pgd->rgd', weights.astype(jnp.bfloat16), pool_values, pre...]
    unnamed x16 -> x12, local copies, waits for them, and re-layouts: 29.2 us -> 6.6 us
    reduce_sum x4 -> x0, other arithmetic: 6.29 us -> none  [the longest x2 3.69 us: body(): squares = jnp.sum(hidden_grid * hidden_grid, axis=(0, 3))]
  transfers between devices with their start and end apart: 5 -> 0, of which waited for: 5 -> 0; matrix products, arithmetic and copies ran while one was open for 1% -> 0% of each run, Pallas kernels for 0% -> 0%
where the time goes in v1:
time: 134 us; the launch traced here: 133 us
  Pallas kernels  118 us (88%)
  local copies, waits for them, and re-layouts  9.15 us (7%)
  other arithmetic  4.94 us (4%)
    pallas_call x1, Pallas kernels, layer_local(): pl.pallas_call(layer_kernel, out_shape=(jax.ShapeDtypeStruct((quarter, wi...  107 us
    pallas_call x1, Pallas kernels, attend_local(): pl.pallas_call(attend_kernel, grid=(width // wide,), in_specs=[slots, slo...  11.5 us
    unnamed x12, local copies, waits for them, and re-layouts  6.6 us

profile of v1, /device:TPU:0, one launch (start us, length us, event | category | flops | bytes accessed | tf_op | source)
XLA Modules:
  0.0 132.9 jit_solution(12226222992297927795)
XLA Ops:
  0.6 0.0 copy-start
  0.7 0.8 compare_select_fusion.1
  1.5 0.8 compare_and_fusion
  2.3 1.5 %gather_fusion = s32[64]{0:T(128)S(1)} fusion(s32[512]{0:T(512)} %param.18, s32[1024]{0:T(1024)S(1)} %pad_clamp_fusion.1), kind=kCustom, calls=%fused_computation | custom fusion | bytes 768 | tf_op jit(solution)/shard_map/jit(_take)/gather | solution.py:537
  3.7 0.8 fusion.1
  4.5 1.3 reshape.36
  5.8 0.1 copy.17
  5.9 0.1 broadcast_in_dim.32.en_ref
  6.0 0.1 reduce
  6.1 0.1 copy.18.st_ref
  6.2 0.2 fusion
  6.4 0.1 pad_maximum_fusion
  6.5 0.0 copy-start.1
  6.5 0.9 copy-done.1
  7.4 0.9 copy-done.2
  8.4 0.9 copy-done.3
  9.3 11.5 %shard_map.140.att_ref = bf16[64,1280]{1,0:T(8,128)(2,1)S(1)} custom-call(bf16[64,1280]{1,0:T(8,128)(2,1)S(1)} %copy-done.1, bf16[64,1280]{1,0:T(8,128)(2,1)S(1)} %copy-done.2, bf16[64,1280]{1,0:T(8,128)(2,1)S(1)} %copy-done.3, bf16[3536,1280]{1,0:T(8,128)(2,1)} %kp_ref.1, bf16[3536,1280]{1,0:T(8,128)(2,1)} %vp_ref.1, ...), custom_call_target="tpu_custom_call" | custom-call | flops 1158676480 | bytes 18104320 | tf_op jit(solution)/shard_map/pallas_call | solution.py:95
  20.8 0.0 copy-start.4
  20.8 0.7 copy-done.4
  21.5 0.9 gather_fusion.1
  22.4 0.8 broadcast_select_fusion.res_ref
  23.1 106.5 %shard_map.141 = (bf16[128,640]{1,0:T(8,128)(2,1)}, bf16[64,1280]{1,0:T(8,128)(2,1)}) custom-call(bf16[64,1280]{1,0:T(8,128)(2,1)} %copy-done.4, bf16[128,640]{1,0:T(8,128)(2,1)} %broadcast_select_fusion.res_ref, f32[8,1,640]{2,1,0:T(1,128)} %bitcast.6, bf16[1280,640]{1,0:T(8,128)(2,1)} %out_hbm.1, bf16[432,5120]{1,0:T(8,128)(2,1)} %bitcast.8, ...), custom_call_target="tpu_custom_call" | custom-call | flops 7633633280 | bytes 14909440 | tf_op jit(solution)/shard_map/pallas_call | solution.py:447
  129.7 1.6 %copy.21 = bf16[128,640]{1,0:T(8,128)(2,1)} copy(bf16[128,640]{1,0:T(8,128)(2,1)} %get-tuple-element.13) | data formatting | bytes 327680
  131.3 1.6 %copy.22 = bf16[64,1280]{1,0:T(8,128)(2,1)} copy(bf16[64,1280]{1,0:T(8,128)(2,1)} %get-tuple-element.14) | data formatting | bytes 327680
  (7 shorter events, 0.0 us)
Async XLA Ops:
  0.6 20.9 %copy-start = (bf16[512,640]{1,0:T(8,128)(2,1)S(1)}, bf16[512,640]{1,0:T(8,128)(2,1)}, u32[]{:S(2)}) copy-start(bf16[512,640]{1,0:T(8,128)(2,1)} %param.20) | copy-start | bytes 1966084
  6.5 0.9 copy-start.1
  7.4 0.9 copy-start.2
  8.4 0.9 copy-start.3
  20.8 0.7 copy-start.4

commit v2 on v1

--- a/solution.py
+++ b/solution.py
@@ -19,23 +19,27 @@
     return (jnp.cos(angles), jnp.sin(angles))
 
 
+def dot_turned(left, right):
+    return lax.dot_general(
+        left, right, (((1,), (1,)), ((), ())), preferred_element_type=jnp.float32
+    )
+
+
 def swap_halves(v):
     half = HD // 2
     return jnp.concatenate([v[:, half:], v[:, :half]], axis=1)
 
 
-def attend_kernel(q_ref, k_ref, v_ref, kp_ref, vp_ref, cos_ref, sin_ref, st_ref, en_ref, out_ref):
+def attend_pair(q_pair, k_pair, v_pair, key_rows, value_rows, cosine, sine, starts, ends):
     scale = HD ** (-0.5)
-    owned = q_ref.shape[0]
-    rows = kp_ref.shape[0]
-    cosine = cos_ref[...]
-    sine = sin_ref[...]
+    owned = q_pair.shape[0]
+    rows = key_rows.shape[0]
     rotated = []
     own = []
     for j in range(2):
         cols = slice(j * HD, (j + 1) * HD)
-        q = q_ref[:, cols].astype(jnp.float32)
-        k = k_ref[:, cols].astype(jnp.float32)
+        q = q_pair[:, cols].astype(jnp.float32)
+        k = k_pair[:, cols].astype(jnp.float32)
         q = (q * cosine + swap_halves(q) * sine).astype(jnp.bfloat16)
         k = (k * cosine + swap_halves(k) * sine).astype(jnp.bfloat16)
         rotated.append(q)
@@ -51,14 +55,9 @@
         axis=0,
     )
     own = jnp.concatenate(own, axis=0)
-    scores = (
-        lax.dot_general(
-            both, kp_ref[...], (((1,), (1,)), ((), ())), preferred_element_type=jnp.float32
-        )
-        * scale
-    )
-    starts = jnp.concatenate([st_ref[...]] * 2, axis=0)
-    ends = jnp.concatenate([en_ref[...]] * 2, axis=0)
+    scores = dot_turned(both, key_rows) * scale
+    starts = jnp.concatenate([starts] * 2, axis=0)
+    ends = jnp.concatenate([ends] * 2, axis=0)
     places = lax.broadcasted_iota(jnp.int32, (2 * owned, rows), 1)
     member = (places >= starts) & (places < ends)
     masked = jnp.where(member, scores, -jnp.inf)
@@ -66,17 +65,50 @@
     weights = jnp.exp(masked - top)
     own_weight = jnp.exp(own - top)
     total = jnp.sum(weights, axis=-1, keepdims=True) + own_weight
-    summed = jnp.dot(
-        weights.astype(jnp.bfloat16), vp_ref[...], preferred_element_type=jnp.float32
-    )
+    summed = jnp.dot(weights.astype(jnp.bfloat16), value_rows, preferred_element_type=jnp.float32)
     own_weight = own_weight.astype(jnp.bfloat16).astype(jnp.float32)
+    heads = []
     for j in range(2):
         cols = slice(j * HD, (j + 1) * HD)
         part = slice(j * owned, (j + 1) * owned)
-        value = v_ref[:, cols].astype(jnp.float32)
-        out_ref[:, cols] = (
-            (summed[part, cols] + own_weight[part] * value) / total[part]
-        ).astype(jnp.bfloat16)
+        value = v_pair[:, cols].astype(jnp.float32)
+        heads.append((summed[part, cols] + own_weight[part] * value) / total[part])
+    return jnp.concatenate(heads, axis=1).astype(jnp.bfloat16)
+
+
+def attend_kernel(q_ref, k_ref, v_ref, kp_ref, vp_ref, cos_ref, sin_ref, st_ref, en_ref, out_ref):
+    out_ref[...] = attend_pair(
+        q_ref[...],
+        k_ref[...],
+        v_ref[...],
+        kp_ref[...],
+        vp_ref[...],
+        cos_ref[...],
+        sin_ref[...],
+        st_ref[...],
+        en_ref[...],
+    )
+
+
+def pick(table_row, chosen):
+    places = lax.broadcasted_iota(jnp.int32, (chosen.shape[0], table_row.shape[1]), 1)
+    hit = places.astype(jnp.float32) == chosen
+    return jnp.sum(jnp.where(hit, table_row, 0.0), axis=1, keepdims=True)
+
+
+def as_column(row):
+    count = row.shape[1]
+    down = lax.broadcasted_iota(jnp.int32, (count, count), 0)
+    across = lax.broadcasted_iota(jnp.int32, (count, count), 1)
+    return jnp.sum(jnp.where(down == across, row, 0.0), axis=1, keepdims=True)
+
+
+def running_starts(column):
+    count = column.shape[0]
+    down = lax.broadcasted_iota(jnp.int32, (count, count), 0)
+    across = lax.broadcasted_iota(jnp.int32, (count, count), 1)
+    row = jnp.sum(jnp.where(down == across, column, 0.0), axis=0, keepdims=True)
+    return jnp.sum(jnp.where(across < down, row, 0.0), axis=1, keepdims=True)
 
 
 def attend_local(query_new, key_new, value_new, key_pool, value_pool, seg_lengths):
@@ -117,16 +149,16 @@
     )
 
 
-def dot_turned(left, right):
-    return lax.dot_general(
-        left, right, (((1,), (1,)), ((), ())), preferred_element_type=jnp.float32
-    )
-
-
 def layer_kernel(
-    att_ref,
-    res_ref,
+    length_ref,
+    slot_ref,
     gain_ref,
+    q_hbm,
+    k_hbm,
+    v_hbm,
+    kp_hbm,
+    vp_hbm,
+    res_hbm,
     out_hbm,
     gate_hbm,
     up_hbm,
@@ -137,6 +169,12 @@
     wg,
     wu,
     wd,
+    q_in,
+    k_in,
+    v_in,
+    kp_in,
+    vp_in,
+    res_in,
     att_all,
     part,
     core_out,
@@ -153,6 +191,13 @@
     x_in,
     z_out,
     z_in,
+    cos_tab,
+    sin_tab,
+    edge_tab,
+    res_rows,
+    n_sem,
+    kp_sem,
+    vp_sem,
     w_sem,
     a_zs,
     a_zr,
@@ -219,38 +264,124 @@
     def arrived(dst, send_sem, recv_sem, device):
         copy(dst, dst, send_sem, recv_sem, device).wait_recv()
 
+    wide = att_all.shape[3]
+    pieces = att_all.shape[0]
+
+    def pair_cols(j):
+        return pl.ds(pl.multiple_of(j * wide, wide), wide)
+
+    def pool_loads(j):
+        slot = j % 2
+        return (
+            pltpu.make_async_copy(kp_hbm.at[:, pair_cols(j)], kp_in.at[slot], kp_sem.at[slot]),
+            pltpu.make_async_copy(vp_hbm.at[:, pair_cols(j)], vp_in.at[slot], vp_sem.at[slot]),
+        )
+
+    new_loads = [
+        pltpu.make_async_copy(src, dst, n_sem.at[i])
+        for i, (src, dst) in enumerate(((q_hbm, q_in), (k_hbm, k_in), (v_hbm, v_in)))
+    ]
     loads = [
         pltpu.make_async_copy(src, dst, w_sem.at[i])
         for i, (src, dst) in enumerate(
-            ((out_hbm, wo), (gate_hbm, wg), (up_hbm, wu), (down_hbm, wd))
+            ((out_hbm, wo), (gate_hbm, wg), (up_hbm, wu), (down_hbm, wd), (res_hbm, res_in))
         )
     ]
-    for load in loads:
-        load.start()
-
     barrier = pltpu.get_barrier_semaphore()
     for device in (to_z[1], to_z[2], to_z[3], to_x, to_y, to_c):
         pl.semaphore_signal(
             barrier, inc=1, device_id=device, device_id_type=pl.DeviceIdType.MESH
         )
+    for load in new_loads:
+        load.start()
+    for j in range(2):
+        for load in pool_loads(j):
+            load.start()
+    for load in (loads[0], loads[4], loads[1], loads[2], loads[3]):
+        load.start()
+
+    length_row = length_ref[...].astype(f32)
+    owned = q_in.shape[0]
+    slot_len = pick(length_row, as_column(slot_ref[pl.ds(r, 1), :].astype(f32)))
+    begin = running_starts(slot_len)
+    starts = begin.astype(jnp.int32)
+    ends = (begin + slot_len).astype(jnp.int32)
+    lane = lax.broadcasted_iota(jnp.int32, (1, HD), 1)
+    freq = (lane % (HD // 2)).astype(f32)
+    angles = slot_len * jnp.exp(freq * (-2.0 * math.log(10000.0) / HD))
+    cosine = jnp.cos(angles)
+    sine = jnp.where(lane < HD // 2, -1.0, 1.0) * jnp.sin(angles)
+    cos_tab[...] = cosine
+    sin_tab[...] = sine
+    edge_tab[0] = jnp.broadcast_to(starts, (owned, HD))
+    edge_tab[1] = jnp.broadcast_to(ends, (owned, HD))
+    part[...] = jnp.zeros_like(part)
+    for load in new_loads:
+        load.wait()
     pl.semaphore_wait(barrier, 6)
 
-    for k in (2, 1, 3):
-        send(att_ref, att_all.at[r], a_zs.at[k], a_zr.at[z], to_z[k])
-    send(att_ref, att_all.at[r], a_xs.at[z], a_xr.at[z], to_x)
-    att_all[r] = att_ref[...]
+    def attention_step(j, carry):
+        @pl.when(j < pieces)
+        def _():
+            for load in pool_loads(j):
+                load.wait()
+            slot = j % 2
+            att_all[j, r] = attend_pair(
+                q_in[:, pair_cols(j)],
+                k_in[:, pair_cols(j)],
+                v_in[:, pair_cols(j)],
+                kp_in[slot],
+                vp_in[slot],
+                cos_tab[...],
+                sin_tab[...],
+                edge_tab[0][:, :1],
+                edge_tab[1][:, :1],
+            )
+
+            @pl.when(j + 2 < pieces)
+            def _():
+                for load in pool_loads(j + 2):
+                    load.start()
+
+            mine = att_all.at[j, r]
+            for k in (1, 3, 2):
+                copy(mine, mine, a_zs.at[j * 4 + k], a_zr.at[j * 4 + z], to_z[k]).start()
+            copy(mine, mine, a_xs.at[j * 4 + z], a_xr.at[j * 4 + z], to_x).start()
+
+        @pl.when((j >= 1) & (j < pieces + 1))
+        def _():
+            p = j - 1
+            for k in (1, 3, 2):
+                q = zs[k]
+                mine = att_all.at[p, q * 2 + x]
+                arrived(mine, a_zs.at[p * 4 + k], a_zr.at[p * 4 + q], to_z[k])
+                copy(mine, mine, a_xs.at[p * 4 + q], a_xr.at[p * 4 + q], to_x).start()
+
+        @pl.when(j >= 2)
+        def _():
+            p = j - 2
+            for k in (0, 1, 3, 2):
+                q = zs[k]
+                arrived(
+                    att_all.at[p, q * 2 + xn], a_xs.at[p * 4 + q], a_xr.at[p * 4 + q], to_x
+                )
+            every = att_all[p].reshape(4 * part.shape[1], wide)
+            depth = pl.ds(pl.multiple_of(p * wide, wide), wide)
+            part[...] += jnp.dot(every, wo[depth, :], preferred_element_type=f32).reshape(
+                part.shape
+            )
+
+        return carry
+
     loads[0].wait()
-    for k in (0, 1, 3, 2):
-        q = zs[k]
-        if k:
-            mine = att_all.at[q * 2 + x]
-            arrived(mine, a_zs.at[k], a_zr.at[q], to_z[k])
-            send(mine, mine, a_xs.at[q], a_xr.at[q], to_x)
-    for k in (0, 1, 3, 2):
-        q = zs[k]
-        arrived(att_all.at[q * 2 + xn], a_xs.at[q], a_xr.at[q], to_x)
-        pair = att_all[pl.ds(q * 2, 2)].reshape(part.shape[1], att_ref.shape[1])
-        part[q] = jnp.dot(pair, wo[...], preferred_element_type=f32)
+    loads[4].wait()
+    for i in range(2):
+        chosen = as_column(slot_ref[pl.ds(h * 2 + i, 1), :].astype(f32))
+        places = lax.broadcasted_iota(jnp.int32, (owned, res_in.shape[0]), 1).astype(f32)
+        hit = jnp.where(places == chosen, 1.0, 0.0).astype(bf16)
+        picked = jnp.dot(hit, res_in[...], preferred_element_type=f32)
+        res_rows[i * owned : (i + 1) * owned, :] = picked
+    lax.fori_loop(0, pieces + 2, attention_step, 0)
 
     for qy in (yn, y):
         core_out[qy] = part[qy * 2 + cn].astype(bf16)
@@ -259,7 +390,7 @@
     y_out[...] = (part[yn * 2 + c] + core_in[yn].astype(f32)).astype(bf16)
     send(y_out, y_in, p_s, p_r, to_y)
     arrived(core_in.at[y], c_s.at[y], c_r.at[y], to_c)
-    total = part[h] + core_in[y].astype(f32) + res_ref[...].astype(f32)
+    total = part[h] + core_in[y].astype(f32) + res_rows[...]
     arrived(y_in, p_s, p_r, to_y)
     mine = (total + y_in[...].astype(f32)).astype(bf16)
     attended_ref[...] = mine
@@ -331,12 +462,12 @@
             gate = up = square = None
             for cx in range(2):
                 at = q * 2 + cx
-                wide = hidden[at, rows, :].astype(f32)
-                power = wide * wide
+                broad = hidden[at, rows, :].astype(f32)
+                power = broad * broad
                 for j in range(width // 128):
                     one = power[:, j * 128 : (j + 1) * 128]
                     square = one if square is None else square + one
-                scaled = (wide * gain_ref[at]).astype(bf16)
+                scaled = (broad * gain_ref[:, pl.ds(pl.multiple_of(at * width, width), width)].astype(f32)).astype(bf16)
                 depth = pl.ds(pl.multiple_of(at * width, width), width)
                 one = dot_turned(scaled, wg[:, depth])
                 gate = one if gate is None else gate + one
@@ -355,7 +486,7 @@
         lax.fori_loop(0, hidden.shape[1] // tall, step, 0)
 
     own_chunk = chunk(z, x, y, c)
-    for k in (2, 1, 3):
+    for k in (1, 3, 2):
         send(own_chunk, own_chunk, h_zs.at[k], h_zr.at[z], to_z[k])
     order = (0, 1, 3, 2)
     first = order[0]
@@ -429,10 +560,39 @@
     for one in sent:
         one.wait_send()
 
-
-def layer_local(attention, rows, out_proj, norm_gain, gate_proj, up_proj, down_proj):
-    owned, feats = attention.shape
-    quarter, width = rows.shape
+    def drain(j, carry):
+        mine = att_all.at[j, r]
+        for k in (1, 3, 2):
+            copy(mine, mine, a_zs.at[j * 4 + k], a_zr.at[j * 4 + z], to_z[k]).wait_send()
+        for k in range(4):
+            q = zs[k]
+            mine = att_all.at[j, q * 2 + x]
+            copy(mine, mine, a_xs.at[j * 4 + q], a_xr.at[j * 4 + q], to_x).wait_send()
+        return carry
+
+    lax.fori_loop(0, pieces, drain, 0)
+
+
+def layer_local(
+    query_new,
+    key_new,
+    value_new,
+    key_pool,
+    value_pool,
+    lengths,
+    slot_request,
+    residual,
+    out_proj,
+    norm_gain,
+    gate_proj,
+    up_proj,
+    down_proj,
+):
+    owned, feats = query_new.shape
+    rows = key_pool.shape[0]
+    slots, width = residual.shape
+    quarter = slots // 4
+    wide = 2 * HD
     gate_proj = gate_proj.T
     up_proj = up_proj.T
     units, hid = gate_proj.shape
@@ -443,21 +603,26 @@
     dma = pltpu.SemaphoreType.DMA
     vmem = pl.BlockSpec(memory_space=pltpu.VMEM)
     hbm = pl.BlockSpec(memory_space=pl.ANY)
-    gain = norm_gain.astype(f32).reshape(blocks, 1, width)
     return pl.pallas_call(
         layer_kernel,
         out_shape=(
             jax.ShapeDtypeStruct((quarter, width), bf16),
             jax.ShapeDtypeStruct((owned, cols), bf16),
         ),
-        in_specs=[vmem, vmem, vmem, hbm, hbm, hbm, hbm],
+        in_specs=[vmem] * 3 + [hbm] * 10,
         out_specs=(vmem, vmem),
         scratch_shapes=[
             pltpu.VMEM(out_proj.shape, bf16),
             pltpu.VMEM(gate_proj.shape, bf16),
             pltpu.VMEM(up_proj.shape, bf16),
             pltpu.VMEM(down_proj.shape, bf16),
-            pltpu.VMEM((8, owned, feats), bf16),
+            pltpu.VMEM((owned, feats), bf16),
+            pltpu.VMEM((owned, feats), bf16),
+            pltpu.VMEM((owned, feats), bf16),
+            pltpu.VMEM((2, rows, wide), bf16),
+            pltpu.VMEM((2, rows, wide), bf16),
+            pltpu.VMEM(residual.shape, bf16),
+            pltpu.VMEM((feats // wide, 8, owned, wide), bf16),
             pltpu.VMEM((4, quarter, width), f32),
             pltpu.VMEM((2, quarter, width), bf16),
             pltpu.VMEM((2, quarter, width), bf16),
@@ -473,11 +638,18 @@
             pltpu.VMEM((4, owned, cols), bf16),
             pltpu.VMEM((4, owned, cols), bf16),
             pltpu.VMEM((4, owned, cols), bf16),
-            dma((4,)),
-            dma((4,)),
-            dma((4,)),
-            dma((4,)),
-            dma((4,)),
+            pltpu.VMEM((owned, HD), f32),
+            pltpu.VMEM((owned, HD), f32),
+            pltpu.VMEM((2, owned, HD), jnp.int32),
+            pltpu.VMEM((quarter, width), f32),
+            dma((3,)),
+            dma((2,)),
+            dma((2,)),
+            dma((5,)),
+            dma((feats // wide * 4,)),
+            dma((feats // wide * 4,)),
+            dma((feats // wide * 4,)),
+            dma((feats // wide * 4,)),
             dma((2,)),
             dma((2,)),
             dma,
@@ -511,7 +683,21 @@
             bytes_accessed=2 * (2 * hid * units + deep * cols + feats * width),
             transcendentals=4 * quarter * units,
         ),
-    )(attention, rows, gain, out_proj, gate_proj, up_proj, down_proj)
+    )(
+        lengths.reshape(1, slots),
+        slot_request.reshape(slots // owned, owned),
+        norm_gain.reshape(1, hid),
+        query_new,
+        key_new,
+        value_new,
+        key_pool,
+        value_pool,
+        residual,
+        out_proj,
+        gate_proj,
+        up_proj,
+        down_proj,
+    )
 
 
 def body(
@@ -532,24 +718,26 @@
     owned = query_new.shape[0]
     req_count = lax.axis_size("req")
     head_count = lax.axis_size("head")
-    first_slot = lax.axis_index("req") * owned
-    my_requests = lax.dynamic_slice_in_dim(slot_request, first_slot, owned, 0)
-    my_lengths = jnp.take(lengths, my_requests, axis=0)
-    attention = attend_local(query_new, key_new, value_new, key_pool, value_pool, my_lengths)
     if (req_count, head_count) == (8, 4):
-        quarter = slot_request.shape[0] // head_count
-        quarter_slots = lax.dynamic_slice_in_dim(
-            slot_request, lax.axis_index("head") * quarter, quarter, 0
-        )
         return layer_local(
-            attention,
-            jnp.take(residual, quarter_slots, axis=0),
+            query_new,
+            key_new,
+            value_new,
+            key_pool,
+            value_pool,
+            lengths,
+            slot_request,
+            residual,
             out_proj,
             norm_gain,
             gate_proj,
             up_proj,
             down_proj,
         )
+    first_slot = lax.axis_index("req") * owned
+    my_requests = lax.dynamic_slice_in_dim(slot_request, first_slot, owned, 0)
+    my_lengths = jnp.take(lengths, my_requests, axis=0)
+    attention = attend_local(query_new, key_new, value_new, key_pool, value_pool, my_lengths)
     partial_sums = jnp.dot(
         lax.all_gather(attention, "req", axis=0, tiled=True),
         out_proj,

time: 134 us -> 115 us (0.86)
  Pallas kernels: 118 us -> 109 us
  other arithmetic: 4.94 us -> 0 us
  local copies, waits for them, and re-layouts: 9.15 us -> 5.86 us
    pallas_call x1 -> x0, Pallas kernels: 11.5 us -> none  [attend_local(): pl.pallas_call(attend_kernel, grid=(width // wide,), in_specs=[slots, slo...]
    unnamed x12 -> x2, local copies, waits for them, and re-layouts: 6.6 us -> 3.19 us
    reshape x0 -> x2, local copies, waits for them, and re-layouts: none -> 2.67 us  [the longest x1 1.35 us: layer_local(): slot_request.reshape(slots // owned, owned)]
    gather x2 -> x0, local copies, waits for them, and re-layouts: 2.36 us -> none  [the longest x1 1.48 us: body(): my_lengths = jnp.take(lengths, my_requests, axis=0)]
    pallas_call x1, Pallas kernels: 107 us -> 109 us  [layer_local(): pl.pallas_call(layer_kernel, out_shape=(jax.ShapeDtypeStruct((quarter, wi...]
    select_n x2 -> x0, other arithmetic: 1.59 us -> none  [the longest x1 0.82 us: body(): my_lengths = jnp.take(lengths, my_requests, axis=0)]
where the time goes in v2:
time: 115 us
  Pallas kernels  109 us (95%)
  local copies, waits for them, and re-layouts  5.86 us (5%)
    pallas_call x1, Pallas kernels, layer_local(): pl.pallas_call(layer_kernel, out_shape=(jax.ShapeDtypeStruct((quarter, wi...  109 us
    unnamed x2, local copies, waits for them, and re-layouts  3.19 us

profile of v2, /device:TPU:0, one launch (start us, length us, event | category | flops | bytes accessed | tf_op | source)
XLA Modules:
  0.0 115.1 jit_solution(16150880629623378058)
XLA Ops:
  0.6 1.3 %reshape.14.slot_ref = s32[8,64]{1,0:T(8,128)} reshape(s32[512]{0:T(512)} %param.19) | data formatting | bytes 4096 | tf_op jit(solution)/shard_map/reshape | solution.py:688
  2.0 1.3 %reshape.15.gain_ref = bf16[1,5120]{1,0:T(2,128)(2,1)} reshape(bf16[5120]{0:T(1024)(128)(2,1)} %param.22) | data formatting | bytes 20480 | tf_op jit(solution)/shard_map/reshape | solution.py:689
  3.3 108.6 %shard_map.140 = (bf16[128,640]{1,0:T(8,128)(2,1)}, bf16[64,1280]{1,0:T(8,128)(2,1)}) custom-call(s32[1,512]{1,0:T(1,128)} %bitcast.5, s32[8,64]{1,0:T(8,128)} %reshape.14.slot_ref, bf16[1,5120]{1,0:T(2,128)(2,1)} %reshape.15.gain_ref, bf16[64,1280]{1,0:T(8,128)(2,1)} %q_hbm.1, bf16[64,1280]{1,0:T(8,128)(2,1)} %k_hbm.1, bf16[64,1280]{1,0:T(8,128)(2,1)} %v_hbm.1, ...), custom_call_target="tpu_custom_call" | custom-call | flops 7633633280 | bytes 14909440 | tf_op jit(solution)/shard_map/pallas_call | solution.py:606
  112.0 1.6 %copy.17 = bf16[128,640]{1,0:T(8,128)(2,1)} copy(bf16[128,640]{1,0:T(8,128)(2,1)} %get-tuple-element.4) | data formatting | bytes 327680
  113.6 1.6 %copy.18 = bf16[64,1280]{1,0:T(8,128)(2,1)} copy(bf16[64,1280]{1,0:T(8,128)(2,1)} %get-tuple-element.5) | data formatting | bytes 327680

commit v3 on v2

--- a/solution.py
+++ b/solution.py
@@ -96,11 +96,8 @@
     return jnp.sum(jnp.where(hit, table_row, 0.0), axis=1, keepdims=True)
 
 
-def as_column(row):
-    count = row.shape[1]
-    down = lax.broadcasted_iota(jnp.int32, (count, count), 0)
-    across = lax.broadcasted_iota(jnp.int32, (count, count), 1)
-    return jnp.sum(jnp.where(down == across, row, 0.0), axis=1, keepdims=True)
+def counting(first, count):
+    return (first + lax.broadcasted_iota(jnp.int32, (count, 1), 0)).astype(jnp.float32)
 
 
 def running_starts(column):
@@ -195,6 +192,7 @@
     sin_tab,
     edge_tab,
     res_rows,
+    gains,
     n_sem,
     kp_sem,
     vp_sem,
@@ -302,7 +300,8 @@
 
     length_row = length_ref[...].astype(f32)
     owned = q_in.shape[0]
-    slot_len = pick(length_row, as_column(slot_ref[pl.ds(r, 1), :].astype(f32)))
+    slot_row = slot_ref[...].astype(f32)
+    slot_len = pick(length_row, pick(slot_row, counting(r * owned, owned)))
     begin = running_starts(slot_len)
     starts = begin.astype(jnp.int32)
     ends = (begin + slot_len).astype(jnp.int32)
@@ -316,6 +315,7 @@
     edge_tab[0] = jnp.broadcast_to(starts, (owned, HD))
     edge_tab[1] = jnp.broadcast_to(ends, (owned, HD))
     part[...] = jnp.zeros_like(part)
+    gains[...] = gain_ref[...].astype(f32)
     for load in new_loads:
         load.wait()
     pl.semaphore_wait(barrier, 6)
@@ -348,6 +348,16 @@
                 copy(mine, mine, a_zs.at[j * 4 + k], a_zr.at[j * 4 + z], to_z[k]).start()
             copy(mine, mine, a_xs.at[j * 4 + z], a_xr.at[j * 4 + z], to_x).start()
 
+        @pl.when(j == pieces)
+        def _():
+            loads[4].wait()
+            for i in range(2):
+                chosen = pick(slot_row, counting((h * 2 + i) * owned, owned))
+                places = lax.broadcasted_iota(jnp.int32, (owned, res_in.shape[0]), 1).astype(f32)
+                hit = jnp.where(places == chosen, 1.0, 0.0).astype(bf16)
+                picked = jnp.dot(hit, res_in[...], preferred_element_type=f32)
+                res_rows[i * owned : (i + 1) * owned, :] = picked
+
         @pl.when((j >= 1) & (j < pieces + 1))
         def _():
             p = j - 1
@@ -356,6 +366,10 @@
                 mine = att_all.at[p, q * 2 + x]
                 arrived(mine, a_zs.at[p * 4 + k], a_zr.at[p * 4 + q], to_z[k])
                 copy(mine, mine, a_xs.at[p * 4 + q], a_xr.at[p * 4 + q], to_x).start()
+
+        @pl.when(j == 2)
+        def _():
+            loads[0].wait()
 
         @pl.when(j >= 2)
         def _():
@@ -373,14 +387,6 @@
 
         return carry
 
-    loads[0].wait()
-    loads[4].wait()
-    for i in range(2):
-        chosen = as_column(slot_ref[pl.ds(h * 2 + i, 1), :].astype(f32))
-        places = lax.broadcasted_iota(jnp.int32, (owned, res_in.shape[0]), 1).astype(f32)
-        hit = jnp.where(places == chosen, 1.0, 0.0).astype(bf16)
-        picked = jnp.dot(hit, res_in[...], preferred_element_type=f32)
-        res_rows[i * owned : (i + 1) * owned, :] = picked
     lax.fori_loop(0, pieces + 2, attention_step, 0)
 
     for qy in (yn, y):
@@ -443,31 +449,38 @@
         arrived(piece, h_bs.at[q], h_br.at[q], to_y)
         to_core(piece, q, 4)
 
-    def collect(k):
+    def collect_near(k):
         q = zs[k]
         from_core(chunk(q, x, y, cn), q, 0)
+        from_core(chunk(q, x, yn, cn), q, 2)
+
+    def collect_far(k):
+        q = zs[k]
         from_core(chunk(q, xn, y, cn), q, 1)
-        from_core(chunk(q, x, yn, cn), q, 2)
         from_core(halved(q, xn, yn, cn, 0), q, 3)
         from_core(halved(q, xn, yn, cn, 1), q, 4)
 
     width = mine.shape[1]
     tall = 2 * quarter
 
-    def multiply(k):
+    def multiply(k, sides=(0, 1)):
         q = zs[k]
 
         def step(i, carry):
             rows = pl.ds(pl.multiple_of(i * tall, tall), tall)
             gate = up = square = None
-            for cx in range(2):
+            for cx in sides:
                 at = q * 2 + cx
                 broad = hidden[at, rows, :].astype(f32)
+                gain = jnp.concatenate(
+                    [gains[pl.ds(at * (width // 128) + j, 1), :] for j in range(width // 128)],
+                    axis=1,
+                )
                 power = broad * broad
                 for j in range(width // 128):
                     one = power[:, j * 128 : (j + 1) * 128]
                     square = one if square is None else square + one
-                scaled = (broad * gain_ref[:, pl.ds(pl.multiple_of(at * width, width), width)].astype(f32)).astype(bf16)
+                scaled = (broad * gain).astype(bf16)
                 depth = pl.ds(pl.multiple_of(at * width, width), width)
                 one = dot_turned(scaled, wg[:, depth])
                 gate = one if gate is None else gate + one
@@ -498,11 +511,14 @@
             spread(order[i + 1])
         diagonal(order[i])
         if i:
-            collect(order[i - 1])
+            collect_near(order[i - 1])
+            collect_far(order[i - 1])
             multiply(order[i - 1])
         finish(order[i])
-    collect(order[3])
-    multiply(order[3])
+    collect_near(order[3])
+    multiply(order[3], (x,))
+    collect_far(order[3])
+    multiply(order[3], (xn,))
 
     def rows_of(q):
         return pl.ds(pl.multiple_of(q * quarter, quarter), quarter)
@@ -642,6 +658,7 @@
             pltpu.VMEM((owned, HD), f32),
             pltpu.VMEM((2, owned, HD), jnp.int32),
             pltpu.VMEM((quarter, width), f32),
+            pltpu.VMEM((hid // 128, 128), f32),
             dma((3,)),
             dma((2,)),
             dma((2,)),
@@ -685,8 +702,8 @@
         ),
     )(
         lengths.reshape(1, slots),
-        slot_request.reshape(slots // owned, owned),
-        norm_gain.reshape(1, hid),
+        slot_request.reshape(1, slots),
+        norm_gain.reshape(hid // 128, 128),
         query_new,
         key_new,
         value_new,
@@ -698,7 +715,6 @@
         up_proj,
         down_proj,
     )
-
 
 def body(
     query_new,

time: 115 us -> 111 us (0.965)
  local copies, waits for them, and re-layouts: 5.86 us -> 3.19 us
  Pallas kernels: 109 us -> 107 us
    reshape x2 -> x0, local copies, waits for them, and re-layouts: 2.67 us -> none  [the longest x1 1.35 us: layer_local(): slot_request.reshape(slots // owned, owned)]
    pallas_call x1, Pallas kernels: 109 us -> 107 us  [layer_local(): pl.pallas_call(layer_kernel, out_shape=(jax.ShapeDtypeStruct((quarter, wi...]
where the time goes in v3:
time: 111 us
  Pallas kernels  107 us (96%)
  local copies, waits for them, and re-layouts  3.19 us (3%)
    pallas_call x1, Pallas kernels, layer_local(): pl.pallas_call(layer_kernel, out_shape=(jax.ShapeDtypeStruct((quarter, wi...  107 us
    unnamed x2, local copies, waits for them, and re-layouts  3.19 us

profile of v3, /device:TPU:0, one launch (start us, length us, event | category | flops | bytes accessed | tf_op | source)
XLA Modules:
  0.0 111.1 jit_solution(5919758908475600071)
XLA Ops:
  0.6 107.3 %shard_map.140 = (bf16[128,640]{1,0:T(8,128)(2,1)}, bf16[64,1280]{1,0:T(8,128)(2,1)}) custom-call(s32[1,512]{1,0:T(1,128)} %bitcast.8, s32[1,512]{1,0:T(1,128)} %bitcast.9, bf16[40,128]{1,0:T(8,128)(2,1)} %bitcast.7, bf16[64,1280]{1,0:T(8,128)(2,1)} %q_hbm.1, bf16[64,1280]{1,0:T(8,128)(2,1)} %k_hbm.1, bf16[64,1280]{1,0:T(8,128)(2,1)} %v_hbm.1, ...), custom_call_target="tpu_custom_call" | custom-call | flops 7633633280 | bytes 14909440 | tf_op jit(solution)/shard_map/pallas_call | solution.py:622
  107.9 1.6 %copy.17 = bf16[128,640]{1,0:T(8,128)(2,1)} copy(bf16[128,640]{1,0:T(8,128)(2,1)} %get-tuple-element.4) | data formatting | bytes 327680
  109.5 1.6 %copy.18 = bf16[64,1280]{1,0:T(8,128)(2,1)} copy(bf16[64,1280]{1,0:T(8,128)(2,1)} %get-tuple-element.5) | data formatting | bytes 327680
